TPU v7x, 256 devices: a whole 4x4x8 slice. The times are simulated.
256 devices in a mesh: mp: 4 (over z_hi, core), fsdp: 64 (over x, y, z_lo).
Axes of the slice: x: 4, y: 4, z: 8 (z_hi: 2, z_lo: 4; z = z_hi * 4 + z_lo), core: 2. Of those that a mesh axis runs over, the one named last changes fastest.
Arguments:
- hidden_in: bfloat16 [4, 49152, 5120], P('mp', 'fsdp'), may hold values from -16 to 16
- gain_in: bfloat16 [4, 5120], P('mp'), may hold values from 0.099609375 to 1.8984375
- w_key: bfloat16 [4, 5120, 512], P('mp', 'fsdp'), may hold values from -0.078125 to 0.078125
- key_gain: bfloat16 [4, 128], P('mp'), may hold values from 0.099609375 to 1.8984375
- partner: int32 [4], replicated, may hold values from 0 to 3, as said below
Outputs:
- grad_key: float32 [4, 5120, 512], P('mp', 'fsdp')
- grad_key_gain: float32 [4, 128], P('mp')
- distill_loss: float32 [4], P('mp')
Inputs may be any that keep to these rules, and one draw needn't show every extreme that they name: partner[m] differs from m.
All inputs are finite; a program needn't handle non-finite values.
Results may differ from a plain program's by a relative error of at most 0.0016.
Values may be sent and summed in bfloat16 or wider, within the bound.
A program may use at most 128 MiB of HBM per device.

v0:
```python
import jax
import jax.numpy as jnp
from jax import lax
from jax.sharding import PartitionSpec as P


def norm_input(hidden, gain):
    values = hidden.astype(jnp.float32)
    scale = lax.rsqrt(jnp.mean(values * values, axis=-1, keepdims=True) + 1e-06)
    return (values * scale * gain.astype(jnp.float32)).astype(jnp.bfloat16)


def norm_keys(keys, gain):
    heads = keys.reshape(keys.shape[0], -1, gain.shape[0])
    inverse = lax.rsqrt(jnp.mean(heads * heads, axis=-1, keepdims=True) + 1e-06)
    return (heads, inverse, heads * inverse * gain.astype(jnp.float32))


def distill_terms(keys_student, keys_teacher, gain_student, gain_teacher):
    heads, inverse, out_student = norm_keys(keys_student, gain_student)
    unused_heads, unused_inverse, out_teacher = norm_keys(keys_teacher, gain_teacher)
    differ = out_student - out_teacher
    loss_sum = jnp.sum(differ * differ)
    upstream = differ / keys_student.shape[1]
    weighted = upstream * gain_student.astype(jnp.float32)
    inner = jnp.sum(weighted * heads, axis=-1, keepdims=True)
    grad_heads = weighted * inverse - heads * inverse * inverse * inverse * inner / heads.shape[-1]
    grad_gain = jnp.sum(upstream * heads * inverse, axis=(0, 1))
    return (loss_sum, grad_heads.reshape(keys_student.shape).astype(jnp.bfloat16), grad_gain)


def local(hidden_in, gain_in, w_key, key_gain, partner):
    own_index = lax.axis_index("mp")
    partner_index = partner[own_index]
    tok_rows = hidden_in.shape[1]
    normed_student = norm_input(hidden_in[0], gain_in[0])
    every_w, every_gain, every_key_gain = (
        lax.all_gather(w_key, "mp", axis=0, tiled=True),
        lax.all_gather(gain_in, "mp", axis=0, tiled=True),
        lax.all_gather(key_gain, "mp", axis=0, tiled=True),
    )
    teach_w = lax.dynamic_index_in_dim(every_w, partner_index, 0, keepdims=False)
    teach_gain = lax.dynamic_index_in_dim(every_gain, partner_index, 0, keepdims=False)
    teach_key_gain = lax.dynamic_index_in_dim(every_key_gain, partner_index, 0, keepdims=False)
    normed_teacher = norm_input(hidden_in[0], teach_gain)
    columns = normed_student
    keys_student = jnp.dot(
        columns,
        lax.all_gather(w_key[0], "fsdp", axis=0, tiled=True),
        preferred_element_type=jnp.float32,
    )
    columns = normed_teacher
    keys_teacher = jnp.dot(
        columns,
        lax.all_gather(teach_w, "fsdp", axis=0, tiled=True),
        preferred_element_type=jnp.float32,
    )
    loss_sum, grad_keys, grad_gain = distill_terms(
        keys_student, keys_teacher, key_gain[0], teach_key_gain
    )
    loss_total, gain_total = lax.psum((loss_sum, grad_gain), "fsdp")
    tokens_all = tok_rows * lax.axis_size("fsdp")
    distill_loss = (loss_total / (tokens_all * w_key.shape[2])).reshape(1)
    columns = normed_student
    grad_rows = lax.psum_scatter(
        lax.dot_general(
            columns, grad_keys, (((0,), (0,)), ((), ())), preferred_element_type=jnp.float32
        ),
        "fsdp",
        scatter_dimension=0,
        tiled=True,
    )
    return (grad_rows[None], gain_total[None], distill_loss)


def solution(mesh):
    return jax.shard_map(
        local,
        mesh=mesh,
        in_specs=(P("mp", "fsdp", None), P("mp", None), P("mp", "fsdp", None), P("mp", None), P()),
        out_specs=(P("mp", "fsdp", None), P("mp", None), P("mp")),
        check_vma=False,
    )
```

profile of v0, /device:TPU:8, one launch (start us, length us, event | category | flops | bytes accessed | tf_op | source)
XLA Modules:
  0.0 1186.6 jit_solution(4204213274397200919)
XLA Ops:
  7.2 0.0 all-gather.9.cloned.1.call-start
  7.2 1.2 dynamic_slice.15
  9.8 12.1 %all_gather.17 = bf16[4,80,512]{2,1,0:T(8,128)(2,1)S(1)} all-gather(bf16[1,80,512]{2,1,0:T(8,128)(2,1)} %param.7), channel_id=1, replica_groups=mesh['mp'=4,'fsdp'=64] {'mp'}, dimensions={0}, use_global_device_ids=true | all-gather | bytes 409600 | tf_op jit(solution)/shard_map/all_gather | solution.py:38
  22.5 0.6 constant_dynamic-slice_fusion.1
  23.2 0.0 all-gather.9.cloned.1.call-update
  23.2 0.0 all-gather.7.cloned.1.call-start
  23.2 0.7 all-gather.7.cloned.1.call-update
  23.9 0.0 reduce-scatter.2.cloned.1.call-start
  24.0 0.8 mul.176
  24.7 9.1 all-gather.3
  33.8 9.4 all-gather.2
  43.3 0.7 bitcast_convert_fusion
  43.9 0.7 broadcast_multiply_fusion
  44.6 4.9 fusion.5
  49.5 335.8 %all-gather.9.cloned.1.call-done = bf16[1,5120,512]{2,1,0:T(8,128)(2,1)} async-done(((bf16[1,80,512]{2,1,0:T(8,128)(2,1)}), bf16[1,5120,512]{2,1,0:T(8,128)(2,1)}) %all-gather.9.cloned.1.call-update) | async-done | bytes 5242896 | tf_op jit(solution)/shard_map/all_gather | solution.py:55
  385.3 7.9 copy.11
  393.2 355.9 %all-gather.7.cloned.1.call-done = bf16[1,5120,512]{2,1,0:T(8,128)(2,1)} async-done(((bf16[1,80,512]{2,1,0:T(8,128)(2,1)}), bf16[1,5120,512]{2,1,0:T(8,128)(2,1)}) %all-gather.7.cloned.1.call-update) | async-done | bytes 5242896 | tf_op jit(solution)/shard_map/all_gather | solution.py:49
  749.1 8.0 copy.10
  757.0 0.0 copy-start
  757.0 0.0 slice-start
  757.0 9.3 multiply_reduce_fusion.3
  766.3 0.0 copy-done
  766.3 0.0 slice-start.1
  766.3 7.1 multiply_reduce_fusion.4
  773.5 1.2 subtract_convert_fusion
  774.7 0.0 slice-done
  774.7 0.0 slice-done.1
  774.7 7.6 fusion.11
  782.3 0.0 reduce-scatter.2.cloned.1.call-update
  782.3 1.5 multiply_reduce_fusion
  783.8 184.5 %all-reduce = (f32[1,128]{1,0:T(1,128)}, f32[]{:T(128)}) all-reduce(f32[1,128]{1,0:T(1,128)S(1)} %bitcast.55, f32[]{:T(128)} %get-tuple-element.3), channel_id=1, replica_groups=mesh['mp'=4,'fsdp'=64] {'fsdp'}, use_global_device_ids=true, to_apply=%region_6.7 | all-reduce | flops 129 | bytes 1032 | tf_op jit(solution)/shard_map/psum | solution.py:61
  968.9 210.0 %reduce-scatter.2.cloned.1.call-done = f32[80,512]{1,0:T(8,128)} async-done(((f32[5120,512]{1,0:T(8,128)}), f32[80,512]{1,0:T(8,128)}) %reduce-scatter.2.cloned.1.call-update) | async-done | bytes 163856 | tf_op jit(solution)/shard_map/reduce_scatter | solution.py:65
  (5 shorter events, 0.1 us)
Async XLA Ops:
  7.2 378.2 %all-gather.9.cloned.1.call-start = ((), (), s32[]{:S(2)}) async-start(), calls=%async_computation.3 | async-start | bytes 5324800 | tf_op jit(solution)/shard_map/all_gather | solution.py:55
  23.2 725.9 %all-gather.7.cloned.1.call-start = ((), (), s32[]{:S(2)}) async-start(), calls=%async_computation.2 | async-start | bytes 5324800 | tf_op jit(solution)/shard_map/all_gather | solution.py:49
  23.9 1155.0 %reduce-scatter.2.cloned.1.call-start = ((), (), s32[]{:S(2)}) async-start(), calls=%async_computation.1 | async-start | bytes 10649600 | tf_op jit(solution)/shard_map/reduce_scatter | solution.py:65
  757.0 9.3 copy-start
  757.0 17.6 %slice-start = ((s8[7864320]{0:T(1024)(128)(4,1)}), s8[4194304]{0:T(1024)(128)(4,1)S(1)}, s32[]{:S(2)}) async-start(s8[7864320]{0:T(1024)(128)(4,1)} %bitcast.44), calls=%async_computation.4 | async-start | bytes 8388608
  766.3 8.4 slice-start.1
Sparse Core Ops, SparseCore 0:
  23.3 361.9 all-gather.8
  387.1 361.8 all-gather.6
  782.4 396.4 reduce-scatter.1
where the time goes:
time: 1200 us; the launch traced here: 1190 us
  waiting for transfers between devices  902 us (75%)
  blocking collectives  215 us (18%)
  matrix products  24 us (2%)
  local copies, waits for them, and re-layouts  17.7 us (1%)
  between operations  17.6 us (1%)
    all_gather x1, waiting for transfers between devices, local(): lax.all_gather(w_key[0], 'fsdp', axis=0, tiled=True)  356 us
    all_gather x1, waiting for transfers between devices, local(): lax.all_gather(teach_w, 'fsdp', axis=0, tiled=True)  336 us
    reduce_scatter x1, waiting for transfers between devices, local(): lax.psum_scatter(lax.dot_general(columns, grad_keys, (((0,), (0,)), ((),...  210 us
    psum x1, blocking collectives, local(): loss_total, gain_total = lax.psum((loss_sum, grad_gain), 'fsdp')  184 us
  transfers between devices with their start and end apart: 3, of which 3 were waited for; matrix products, arithmetic and copies ran while one was open for 1% of the time, Pallas kernels for 0%

commit v1 on v0

v1 whole, which is shorter than its diff:
```python
import jax
import jax.numpy as jnp
from jax import lax
from jax.experimental import pallas as pl
from jax.experimental.pallas import tpu as pltpu
from jax.sharding import PartitionSpec as P

MESH = pl.DeviceIdType.MESH
F32, BF16, I16 = jnp.float32, jnp.bfloat16, jnp.int16
D, KW, HD, TOK, CHUNK = 5120, 512, 128, 768, 80
HALF = KW // 2
SLAB = D // 4
EPS = 1e-6
TOP = 32767.0
ROWS = (pl.ds(0, 32), pl.ds(32, 32), pl.ds(64, 16))
NSEM = 420


def kernel(
    hid, gains, w, partner, grad, stats,
    wall0, wall1, ns, nt, nst, ks, kt, gk, gt, q, sc, g4, stat4,
    r1x, r1y, r1z, s1, acc, q2x, q2y, q2z, r2x, r2y, r2z, s2o, s2,
    q3x, q3y, q3z, r3x, r3y, r3z, s3o, s3, ssem, rsem, lsem,
):
    m, f = lax.axis_index("mp"), lax.axis_index("fsdp")
    x, y = f // 16, (f // 4) % 4
    zl, zh, c = f % 4, m // 2, m % 2
    z = zh * 4 + zl

    def dev(px, py, pz, pc):
        pz = (pz + 8) % 8
        return ((pz // 4) * 2 + pc, (((px + 4) % 4) * 4 + (py + 4) % 4) * 4 + pz % 4)

    def at_x(d):
        return dev(x + d, y, z, c)

    def at_y(d):
        return dev(x, y + d, z, c)

    def at_z(d):
        return dev(x, y, z + d, c)

    def at_line(d):
        return dev(x, y, zh * 4 + (zl + d) % 4, c)

    walls = (wall0, wall1)
    sibling = dev(x, y, z, 1 - c)
    others = (sibling, dev(x, y, z + 4, c), dev(x, y, z + 4, 1 - c))
    slot_of = (zh * 2 + 1 - c, (1 - zh) * 2 + c, (1 - zh) * 2 + 1 - c)

    used = [0]
    pending = []

    def take(n=1):
        used[0] += n
        assert used[0] <= NSEM
        return used[0] - n

    def copy(src, dst, to, si, ri):
        return pltpu.make_async_remote_copy(
            src_ref=src, dst_ref=dst, send_sem=ssem.at[si], recv_sem=rsem.at[ri],
            device_id=to, device_id_type=MESH,
        )

    def send(src, dst, to, ri=None):
        si = take()
        ri = si if ri is None else ri
        one = copy(src, dst, to, si, ri)
        one.start()
        pending.append(one)
        return ri

    def arrived(ref, ri):
        copy(ref, ref, sibling, ri, ri).wait_recv()

    loads = [
        pltpu.make_async_copy(w.at[0, :, pl.ds(HALF * ph, HALF)], walls[ph].at[m, x, y, zl], lsem.at[ph])
        for ph in range(2)
    ]
    for one in loads:
        one.start()
    hidden_loads = [
        pltpu.make_async_copy(hid.at[0, :, pl.ds(SLAB * s, SLAB)], nt.at[s], lsem.at[2 + s]) for s in range(4)
    ]
    for one in hidden_loads:
        one.start()
    barrier = pltpu.get_barrier_semaphore()
    peers = [at_x(d) for d in (1, 2, 3)] + [at_y(d) for d in (1, 2, 3)] + [at_z(1), at_z(-1)]
    peers += [at_line(d) for d in (1, 2, 3)] + list(others)
    for one in peers:
        pl.semaphore_signal(barrier, inc=1, device_id=one, device_id_type=MESH)
    g4[m] = gains[...]
    pl.semaphore_wait(barrier, len(peers))

    def model(zz):
        return (zz // 4) * 2 + c

    def gather(ph):
        back = take(2)

        def chunk(px, py, part):
            return walls[ph].at[m, px, py, zl, ROWS[part]]

        def block(part, zz, lane=None, half=None):
            some = slice(None) if half is None else pl.ds(2 * half, 2)
            mod, low, rows = model(zz), zz % 4, ROWS[part]
            if lane is None:
                return walls[ph].at[mod, some, :, low, rows]
            lane = (lane + 4) % 4
            if part == 0:
                return walls[ph].at[mod, lane, some, low, rows]
            return walls[ph].at[mod, some, lane, low, rows]

        at = (at_x, at_y)
        pos = (x, y)

        first = []
        for part, hop in ((0, at_y), (1, at_x), (2, at_x)):
            mine = chunk(x, y, part)
            first.append([send(mine, mine, hop(d)) for d in (1, 2, 3)])
        yield

        ring = {}
        last = {}

        def z_own(part, lane):
            mine = block(part, z, lane)
            up = send(mine, mine, at_z(1))
            down = send(mine, mine, at_z(-1))
            ring[part] = (up, down)

        def z_step(part, lane, j):
            up, down = ring[part]
            if j < 4:
                for sign, ri in ((-1, up), (1, down)):
                    got = block(part, (z + sign * j + 8) % 8, lane)
                    arrived(got, ri)
                half = {1: None, 2: None, 3: 0}[j]
                one = block(part, (z - j + 8) % 8, lane, half)
                up = send(one, one, at_z(1))
                half = {1: None, 2: None, 3: 1}[j]
                one = block(part, (z + j) % 8, lane, half)
                down = send(one, one, at_z(-1))
                ring[part] = (up, down)
            else:
                arrived(block(part, (z + 4) % 8, lane, 0), up)
                arrived(block(part, (z + 4) % 8, lane, 1), down)

        def l_own(part, j):
            one = block(part, (z + j + 8) % 8, pos[part])
            last[part, j] = (send(one, one, at[part](1)), send(one, one, at[part](-1)))

        def l_pass(part, j):
            zz = (z + j + 8) % 8
            up, down = last[part, j]
            arrived(block(part, zz, pos[part] - 1), up)
            one = block(part, zz, pos[part] - 1, 0)
            up = send(one, one, at[part](1))
            arrived(block(part, zz, pos[part] + 1), down)
            one = block(part, zz, pos[part] + 1, 1)
            down = send(one, one, at[part](-1))
            last[part, j] = (up, down)

        def hand_over(part, j):
            zz = (z + j + 8) % 8
            one = block(part, zz)
            send(one, one, sibling, back + zz // 4)

        def l_end(part, j):
            zz = (z + j + 8) % 8
            up, down = last[part, j]
            arrived(block(part, zz, pos[part] + 2, 0), up)
            arrived(block(part, zz, pos[part] + 2, 1), down)
            hand_over(part, j)

        for d in (1, 2, 3):
            arrived(chunk(x, (y - d + 4) % 4, 0), first[0][d - 1])
        z_own(0, x)
        l_own(0, 0)
        for d in (1, 2, 3):
            arrived(chunk((x - d + 4) % 4, y, 1), first[1][d - 1])
        z_own(1, y)
        l_own(1, 0)
        for d in (1, 2, 3):
            arrived(chunk((x - d + 4) % 4, y, 2), first[2][d - 1])
        mine = walls[ph].at[m, :, y, zl, ROWS[2]]
        second = [send(mine, mine, at_y(d)) for d in (1, 2, 3)]
        yield
        for j in range(1, 5):
            for part in (0, 1):
                z_step(part, pos[part], j)
                for sign in (-1, 1) if j < 4 else (1,):
                    l_own(part, sign * j)
                yield
            if j == 1:
                for d in (1, 2, 3):
                    arrived(walls[ph].at[m, :, (y - d + 4) % 4, zl, ROWS[2]], second[d - 1])
                z_own(2, None)
                hand_over(2, 0)
            else:
                z_step(2, None, j - 1)
                hand_over(2, j - 1)
                hand_over(2, 1 - j)
            yield
            for part in (0, 1):
                for sign in (-1, 1) if j > 1 else (1,):
                    l_pass(part, sign * (j - 1))
                if j > 1:
                    for sign in (-1, 1) if j > 2 else (1,):
                        l_end(part, sign * (j - 2))
                yield
        for part in (0, 1):
            l_pass(part, 4)
            for sign in (-1, 1):
                l_end(part, sign * 3)
            yield
        z_step(2, None, 4)
        hand_over(2, 4)
        for part in (0, 1):
            l_end(part, 4)
        yield
        for h in range(2):
            arrived(walls[ph].at[h * 2 + 1 - c], back + h)

    def teacher():
        return partner[m]

    got_gain = []

    def share_gains():
        for to in others:
            got_gain.append(send(g4.at[m], g4.at[m], to))

    def wait_inputs():
        for slot, ri in zip(slot_of, got_gain):
            arrived(g4.at[slot], ri)
        for one in hidden_loads:
            one.wait()

    def prep(t):
        def rows16(i, carry):
            rows = pl.ds(pl.multiple_of(t * 128 + i * 16, 16), 16)
            total = jnp.zeros((16, 1), F32)
            for s in range(4):
                v = nt[s, rows, :].astype(F32)
                total = total + jnp.sum(v * v, axis=-1, keepdims=True)
            scale = lax.rsqrt(total / D + EPS)
            p = teacher()
            for s in range(4):
                v = nt[s, rows, :].astype(F32) * scale
                ns[s, rows, :] = (v * g4[m, s]).astype(BF16)
                nt[s, rows, :] = (v * g4[p, s]).astype(BF16)
            return carry

        lax.fori_loop(0, 8, rows16, 0)

        def turn(s, carry):
            nst[s, :, pl.ds(t * 128, 128)] = ns[s, pl.ds(t * 128, 128), :].T
            return carry

        lax.fori_loop(0, 4, turn, 0)

    def keys(ph, which, s):
        left, out = ((ns, ks), (nt, kt))[which]
        who = m if which == 0 else teacher()
        right = walls[ph][who, s].reshape(SLAB, HALF)
        part = jnp.dot(left[s], right, preferred_element_type=F32)
        if s == 0:
            out[...] = part
        else:
            out[...] += part

    def distill(ph):
        p = teacher()

        def tile(i, carry):
            loss, ggain = carry
            rows = pl.ds(pl.multiple_of(i * 64, 64), 64)
            own_gain, far_gain = g4[m, 4][:, :HD], g4[p, 4][:, :HD]
            for h in range(2):
                cols = pl.ds(h * HD, HD)
                a, b = ks[rows, cols], kt[rows, cols]
                inv_a = lax.rsqrt(jnp.sum(a * a, axis=-1, keepdims=True) / HD + EPS)
                inv_b = lax.rsqrt(jnp.sum(b * b, axis=-1, keepdims=True) / HD + EPS)
                differ = a * inv_a * own_gain - b * inv_b * far_gain
                loss = loss + jnp.sum(differ * differ, axis=0, keepdims=True)
                up = differ / KW
                weighted = up * own_gain
                inner = jnp.sum(weighted * a, axis=-1, keepdims=True)
                g = weighted * inv_a - a * (inv_a * inv_a * inv_a * inner / HD)
                gk[rows, cols] = g.astype(BF16)
                ggain = ggain + jnp.sum(up * a * inv_a, axis=0, keepdims=True)
            return loss, ggain

        zero = jnp.zeros((1, HD), F32)
        loss, ggain = lax.fori_loop(0, TOK // 64, tile, (zero, zero))
        if ph == 0:
            stat4[0, 0:1] = loss
            stat4[0, 1:2] = ggain
        else:
            stat4[0, 0:1] += loss
            stat4[0, 1:2] += ggain

    base1 = [take(9) for _ in range(2)]
    base1s = [take(9) for _ in range(2)]

    def quantize(read, write, n):
        def most(i, top):
            v = jnp.abs(read(i))
            return jnp.maximum(top, jnp.max(v.reshape(-1, HALF), axis=0, keepdims=True))

        top = lax.fori_loop(0, n, most, jnp.full((1, HALF), 1e-30, F32))
        factor = TOP / top

        def store(i, carry):
            write(i, jnp.round(read(i) * factor).astype(jnp.int32).astype(I16))
            return carry

        lax.fori_loop(0, n, store, 0)
        return top / TOP

    def grads(ph, d):
        s = (x + d) % 4
        gt[...] = jnp.dot(nst[s], gk[...], preferred_element_type=F32).reshape(4, 4, CHUNK, HALF)

        def read(i):
            return gt[i // 4, i % 4]

        def write(i, v):
            q[ph, s, i // 4, i % 4] = v

        sc[ph, s] = quantize(read, write, 16)
        if d < 4:
            one = copy(q.at[ph, s, :, :, ROWS[0]], r1x.at[ph, d - 1], at_x(d), base1[ph] + d - 1, base1[ph] + d - 1)
            one.start()
            pending.append(one)

    def grads_send(ph):
        for d in (1, 2, 3):
            k = base1[ph] + 2 + d
            one = copy(q.at[ph, :, (y + d) % 4, :, ROWS[1]], r1y.at[ph, d - 1], at_y(d), k, k)
            one.start()
            pending.append(one)
            k = base1[ph] + 5 + d
            one = copy(q.at[ph, :, :, (zl + d) % 4, ROWS[2]], r1z.at[ph, d - 1], at_line(d), k, k)
            one.start()
            pending.append(one)
        for a, hop in enumerate((at_x, at_y, at_line)):
            for d in (1, 2, 3):
                k = base1s[ph] + 3 * a + d - 1
                one = copy(sc.at[ph], s1.at[ph, a, d - 1], hop(d), k, k)
                one.start()
                pending.append(one)

    def wait1(ph, a, ref):
        for d in range(3):
            arrived(ref.at[ph, d], base1[ph] + 3 * a + d)
            arrived(s1.at[ph, a, d], base1s[ph] + 3 * a + d)

    def i2f(v):
        return v.astype(jnp.int32).astype(F32)

    def stage2(ph):
        ids = {}
        wait1(ph, 0, r1x)

        def add0(i, carry):
            a, b = i // 4, i % 4
            v = i2f(q[ph, x, a, b, ROWS[0]]) * sc[ph, x]
            for d in range(3):
                v = v + i2f(r1x[ph, d, a, b]) * s1[ph, 0, d, x]
            acc[a, b] = v
            return carry

        lax.fori_loop(0, 16, add0, 0)

        def write0(i, v):
            q2x[ph, i // 4, i % 4] = v

        s2o[ph, 0] = quantize(lambda i: acc[i // 4, i % 4], write0, 16)
        for d in (1, 2, 3):
            ids[0, d] = (
                send(q2x.at[ph, (y + d) % 4], r2x.at[ph, d - 1], at_y(d)),
                send(s2o.at[ph, 0], s2.at[ph, 0, d - 1], at_y(d)),
            )
        wait1(ph, 1, r1y)

        def add1(i, carry):
            a, b = i // 4, i % 4
            v = i2f(q[ph, a, y, b, ROWS[1]]) * sc[ph, a]
            for d in range(3):
                v = v + i2f(r1y[ph, d, a, b]) * s1[ph, 1, d, a]
            acc[a, b] = v
            return carry

        lax.fori_loop(0, 16, add1, 0)

        def write1(i, v):
            q2y[ph, i // 4, i % 4] = v

        s2o[ph, 1] = quantize(lambda i: acc[i // 4, i % 4], write1, 16)
        for d in (1, 2, 3):
            ids[1, d] = (
                send(q2y.at[ph, (x + d) % 4], r2y.at[ph, d - 1], at_x(d)),
                send(s2o.at[ph, 1], s2.at[ph, 1, d - 1], at_x(d)),
            )
        wait1(ph, 2, r1z)

        def add2(i, carry):
            a, b = i // 4, i % 4
            v = i2f(q[ph, a, b, zl, ROWS[2]]) * sc[ph, a]
            for d in range(3):
                v = v + i2f(r1z[ph, d, a, b]) * s1[ph, 2, d, a]
            acc[a, b, 0:16] = v
            return carry

        lax.fori_loop(0, 16, add2, 0)

        def write2(i, v):
            q2z[ph, i // 4, i % 4] = v

        s2o[ph, 2] = quantize(lambda i: acc[i // 4, i % 4, 0:16], write2, 16)
        for d in (1, 2, 3):
            ids[2, d] = (
                send(q2z.at[ph, (x + d) % 4], r2z.at[ph, d - 1], at_x(d)),
                send(s2o.at[ph, 2], s2.at[ph, 2, d - 1], at_x(d)),
            )
        return ids

    def stage3(ph, ids):
        out = {}
        for a, (own, got, mid, pos, hop, n) in enumerate((
            (q2x.at[ph, y], r2x, q3x, zl, at_line, 32),
            (q2y.at[ph, x], r2y, q3y, zl, at_line, 32),
            (q2z.at[ph, x], r2z, q3z, y, at_y, 16),
        )):
            for d in (1, 2, 3):
                arrived(got.at[ph, d - 1], ids[a, d][0])
                arrived(s2.at[ph, a, d - 1], ids[a, d][1])
            for b in range(4):
                v = i2f(own[b]) * s2o[ph, a]
                for d in range(3):
                    v = v + i2f(got[ph, d, b]) * s2[ph, a, d]
                acc[0, b, 0:n] = v

            def write(i, v, mid=mid):
                mid[ph, i] = v

            s3o[ph, a] = quantize(lambda i, n=n: acc[0, i, 0:n], write, 4)
            into = (r3x, r3y, r3z)[a]
            for d in (1, 2, 3):
                out[a, d] = (
                    send(mid.at[ph, (pos + d) % 4], into.at[ph, d - 1], hop(d)),
                    send(s3o.at[ph, a], s3.at[ph, a, d - 1], hop(d)),
                )
        return out

    def finish(ph, ids):
        for a, (own, got, n, row) in enumerate((
            (q3x.at[ph, zl], r3x, 32, 0), (q3y.at[ph, zl], r3y, 32, 32), (q3z.at[ph, y], r3z, 16, 64),
        )):
            v = i2f(own[...]) * s3o[ph, a]
            for d in (1, 2, 3):
                arrived(got.at[ph, d - 1], ids[a, d][0])
                arrived(s3.at[ph, a, d - 1], ids[a, d][1])
                v = v + i2f(got[ph, d - 1]) * s3[ph, a, d - 1]
            grad[row : row + n, HALF * ph : HALF * ph + HALF] = v

    def stat_send(a, hop):
        return [send(stat4.at[4 * a], stat4.at[4 * a + d], hop(d)) for d in (1, 2, 3)]

    def stat_add(a, ids):
        v = stat4[4 * a]
        for d in (1, 2, 3):
            arrived(stat4.at[4 * a + d], ids[d - 1])
            v = v + stat4[4 * a + d]
        return v

    def together(events, pieces):
        pieces = list(pieces)
        for _ in events:
            if pieces:
                pieces.pop(0)()
        for one in pieces:
            one()

    for one in loads:
        one.wait()
    one_a, one_b = gather(0), gather(1)
    next(one_a)
    share_gains()
    next(one_a)
    next(one_b)
    stat4[0] = jnp.zeros((8, HD), F32)
    together(one_a, [wait_inputs] + [lambda t=t: prep(t) for t in range(6)] + [lambda: next(one_b)])

    def work(ph):
        for which in (0, 1):
            for s in range(4):
                yield lambda which=which, s=s: keys(ph, which, s)
        yield lambda: distill(ph)
        for d in (1, 2, 3, 4):
            yield lambda d=d: grads(ph, d)
        yield lambda: grads_send(ph)

    together(one_b, work(0))
    for one in work(1):
        one()
    sid = stat_send(0, at_x)
    ids_a = stage2(0)
    stat4[4] = stat_add(0, sid)
    sid = stat_send(1, at_y)
    ids_a = stage3(0, ids_a)
    ids_b = stage2(1)
    stat4[8] = stat_add(1, sid)
    sid = stat_send(2, at_line)
    finish(0, ids_a)
    ids_b = stage3(1, ids_b)
    total = stat_add(2, sid)
    loss = jnp.sum(total[0:1], axis=-1, keepdims=True) / float(TOK * 64 * KW)
    stats[...] = jnp.concatenate([jnp.broadcast_to(loss, (1, HD)), total[1:8]], axis=0)
    finish(1, ids_b)
    for one in pending:
        one.wait_send()


def local(hidden_in, gain_in, w_key, key_gain, partner):
    gains = jnp.concatenate(
        [gain_in.astype(F32).reshape(4, 1, SLAB), jnp.pad(key_gain.astype(F32), ((0, 0), (0, SLAB - HD))).reshape(1, 1, SLAB)]
    )
    vmem, dma = pltpu.VMEM, pltpu.SemaphoreType.DMA
    grad, stats = pl.pallas_call(
        kernel,
        out_shape=(jax.ShapeDtypeStruct((CHUNK, KW), F32), jax.ShapeDtypeStruct((8, HD), F32)),
        in_specs=[
            pl.BlockSpec(memory_space=pl.ANY),
            pl.BlockSpec(memory_space=pltpu.VMEM),
            pl.BlockSpec(memory_space=pl.ANY),
            pl.BlockSpec(memory_space=pltpu.SMEM),
        ],
        out_specs=(pl.BlockSpec(memory_space=pltpu.VMEM), pl.BlockSpec(memory_space=pltpu.VMEM)),
        scratch_shapes=[
            vmem((4, 4, 4, 4, CHUNK, HALF), BF16),
            vmem((4, 4, 4, 4, CHUNK, HALF), BF16),
            vmem((4, TOK, SLAB), BF16),
            vmem((4, TOK, SLAB), BF16),
            vmem((4, SLAB, TOK), BF16),
            vmem((TOK, HALF), F32),
            vmem((TOK, HALF), F32),
            vmem((TOK, HALF), BF16),
            vmem((4, 4, CHUNK, HALF), F32),
            vmem((2, 4, 4, 4, CHUNK, HALF), I16),
            vmem((2, 4, 1, HALF), F32),
            vmem((4, 5, 1, SLAB), F32),
            vmem((12, 8, HD), F32),
            vmem((2, 3, 4, 4, 32, HALF), I16),
            vmem((2, 3, 4, 4, 32, HALF), I16),
            vmem((2, 3, 4, 4, 16, HALF), I16),
            vmem((2, 3, 3, 4, 1, HALF), F32),
            vmem((4, 4, 32, HALF), F32),
            vmem((2, 4, 4, 32, HALF), I16),
            vmem((2, 4, 4, 32, HALF), I16),
            vmem((2, 4, 4, 16, HALF), I16),
            vmem((2, 3, 4, 32, HALF), I16),
            vmem((2, 3, 4, 32, HALF), I16),
            vmem((2, 3, 4, 16, HALF), I16),
            vmem((2, 3, 1, HALF), F32),
            vmem((2, 3, 3, 1, HALF), F32),
            vmem((2, 4, 32, HALF), I16),
            vmem((2, 4, 32, HALF), I16),
            vmem((2, 4, 16, HALF), I16),
            vmem((2, 3, 32, HALF), I16),
            vmem((2, 3, 32, HALF), I16),
            vmem((2, 3, 16, HALF), I16),
            vmem((2, 3, 1, HALF), F32),
            vmem((2, 3, 3, 1, HALF), F32),
            dma((NSEM,)),
            dma((NSEM,)),
            dma((8,)),
        ],
        compiler_params=pltpu.CompilerParams(
            collective_id=0, has_side_effects=True, vmem_limit_bytes=63 * 2**20
        ),
        cost_estimate=pl.CostEstimate(flops=12 * 10**9, bytes_accessed=10**7, transcendentals=0),
    )(hidden_in, gains, w_key, partner)
    return (grad[None], stats[1:2], stats[0, 0:1])


def solution(mesh):
    return jax.shard_map(
        local,
        mesh=mesh,
        in_specs=(P("mp", "fsdp", None), P("mp", None), P("mp", "fsdp", None), P("mp", None), P()),
        out_specs=(P("mp", "fsdp", None), P("mp", None), P("mp")),
        check_vma=False,
    )
```

time: 1200 us -> 150 us (0.12); the launches traced: 1190 us -> 149 us
  waiting for transfers between devices: 902 us -> 0 us
  blocking collectives: 215 us -> 0 us
  Pallas kernels: 0 us -> 142 us
  matrix products: 24 us -> 0 us
  between operations: 17.6 us -> 0.64 us
  local copies, waits for them, and re-layouts: 17.7 us -> 4.64 us
    all_gather x2 -> x0, waiting for transfers between devices: 692 us -> none  [the longest x1 356 us: local(): lax.all_gather(w_key[0], 'fsdp', axis=0, tiled=True)]
    reduce_scatter x1 -> x0, waiting for transfers between devices: 210 us -> none  [local(): lax.psum_scatter(lax.dot_general(columns, grad_keys, (((0,), (0,)), ((),...]
    psum x1 -> x0, blocking collectives: 184 us -> none  [local(): loss_total, gain_total = lax.psum((loss_sum, grad_gain), 'fsdp')]
    pallas_call x0 -> x1, Pallas kernels: none -> 142 us  [local(): pl.pallas_call(kernel, out_shape=(jax.ShapeDtypeStruct((CHUNK, KW), F32),...]
    all_gather x3 -> x0, blocking collectives: 30.6 us -> none  [the longest x1 12.1 us: local(): lax.all_gather(w_key, 'mp', axis=0, tiled=True)]
    dot_general x3 -> x0, matrix products: 24 us -> none  [the longest x1 9.25 us: local(): jnp.dot(columns, lax.all_gather(teach_w, 'fsdp', axis=0, tiled=True), pre...]
    dot_general x2 -> x0, local copies, waits for them, and re-layouts: 15.8 us -> none  [the longest x1 7.98 us: local(): jnp.dot(columns, lax.all_gather(w_key[0], 'fsdp', axis=0, tiled=True), pr...]
  transfers between devices with their start and end apart: 3 -> 0, of which waited for: 3 -> 0; matrix products, arithmetic and copies ran while one was open for 1% -> 0% of each run, Pallas kernels for 0% -> 0%
where the time goes in v1:
time: 150 us; the launch traced here: 149 us
  Pallas kernels  142 us (95%)
  local copies, waits for them, and re-layouts  4.64 us (3%)
    pallas_call x1, Pallas kernels, local(): pl.pallas_call(kernel, out_shape=(jax.ShapeDtypeStruct((CHUNK, KW), F32),...  142 us

profile of v1, /device:TPU:8, one launch (start us, length us, event | category | flops | bytes accessed | tf_op | source)
XLA Modules:
  0.0 148.9 jit_solution(9001517813473535213)
XLA Ops:
  0.6 0.7 pad_bitcast_fusion
  1.3 1.4 maximum_convert_fusion.gains
  2.7 142.3 %shard_map.76 = (f32[80,512]{1,0:T(8,128)}, f32[8,128]{1,0:T(8,128)}) custom-call(bf16[1,768,5120]{2,1,0:T(8,128)(2,1)} %hid.1, f32[5,1,1280]{2,1,0:T(1,128)} %maximum_convert_fusion.gains, bf16[1,80,512]{2,1,0:T(8,128)(2,1)} %w.1, s32[4]{0:T(128)} %partner.1), custom_call_target="tpu_custom_call" | custom-call | flops 12000000000 | bytes 10000000 | tf_op jit(solution)/shard_map/pallas_call | solution.py:532
  144.9 1.2 slice.7
  146.1 1.2 slice.6
  147.3 1.6 %copy.9 = f32[1,80,512]{2,1,0:T(8,128)} copy(f32[1,80,512]{2,1,0:T(8,128)} %bitcast.5) | data formatting | bytes 327680

commit v2 on v1

--- a/solution.py
+++ b/solution.py
@@ -13,12 +13,15 @@
 EPS = 1e-6
 TOP = 32767.0
 ROWS = (pl.ds(0, 32), pl.ds(32, 32), pl.ds(64, 16))
-NSEM = 420
+NSEM = 250
+NSEND = 96
+LEAD = 10
+MAGIC = 12582912.0
 
 
 def kernel(
-    hid, gains, w, partner, grad, stats,
-    wall0, wall1, ns, nt, nst, ks, kt, gk, gt, q, sc, g4, stat4,
+    hid, gain, key_gain, w, partner, grad, stats,
+    wall0, wall1, ns, nt, nst, ks, kt, gk, q, sc, g4, stat4,
     r1x, r1y, r1z, s1, acc, q2x, q2y, q2z, r2x, r2y, r2z, s2o, s2,
     q3x, q3y, q3z, r3x, r3y, r3z, s3o, s3, ssem, rsem, lsem,
 ):
@@ -48,8 +51,8 @@
     others = (sibling, dev(x, y, z + 4, c), dev(x, y, z + 4, 1 - c))
     slot_of = (zh * 2 + 1 - c, (1 - zh) * 2 + c, (1 - zh) * 2 + 1 - c)
 
-    used = [0]
-    pending = []
+    used, sent = [0], [0]
+    pending = {}
 
     def take(n=1):
         used[0] += n
@@ -63,15 +66,18 @@
         )
 
     def send(src, dst, to, ri=None):
-        si = take()
-        ri = si if ri is None else ri
+        si = sent[0] % NSEND
+        sent[0] += 1
+        ri = take() if ri is None else ri
+        if si in pending:
+            pending[si].wait_send()
         one = copy(src, dst, to, si, ri)
         one.start()
-        pending.append(one)
+        pending[si] = one
         return ri
 
     def arrived(ref, ri):
-        copy(ref, ref, sibling, ri, ri).wait_recv()
+        copy(ref, ref, sibling, 0, ri).wait_recv()
 
     loads = [
         pltpu.make_async_copy(w.at[0, :, pl.ds(HALF * ph, HALF)], walls[ph].at[m, x, y, zl], lsem.at[ph])
@@ -89,7 +95,10 @@
     peers += [at_line(d) for d in (1, 2, 3)] + list(others)
     for one in peers:
         pl.semaphore_signal(barrier, inc=1, device_id=one, device_id_type=MESH)
-    g4[m] = gains[...]
+    for s in range(4):
+        g4[m, s] = gain[:, SLAB * s : SLAB * s + SLAB].astype(F32)
+    g4[m, 4] = jnp.zeros((1, SLAB), F32)
+    g4[m, 4, :, 0:HD] = key_gain[...].astype(F32)
     pl.semaphore_wait(barrier, len(peers))
 
     def model(zz):
@@ -301,158 +310,97 @@
             stat4[0, 0:1] += loss
             stat4[0, 1:2] += ggain
 
-    base1 = [take(9) for _ in range(2)]
-    base1s = [take(9) for _ in range(2)]
-
-    def quantize(read, write, n):
-        def most(i, top):
-            v = jnp.abs(read(i))
-            return jnp.maximum(top, jnp.max(v.reshape(-1, HALF), axis=0, keepdims=True))
-
-        top = lax.fori_loop(0, n, most, jnp.full((1, HALF), 1e-30, F32))
-        factor = TOP / top
-
-        def store(i, carry):
-            write(i, jnp.round(read(i) * factor).astype(jnp.int32).astype(I16))
-            return carry
-
-        lax.fori_loop(0, n, store, 0)
-        return top / TOP
+    base1 = [take(6) for _ in range(2)]
+
+    def to_i16(v):
+        return ((v + MAGIC) - MAGIC).astype(jnp.int32).astype(I16)
+
+    def top_of(v):
+        return jnp.max(jnp.abs(v).reshape(-1, HALF), axis=0, keepdims=True)
 
     def grads(ph, d):
         s = (x + d) % 4
-        gt[...] = jnp.dot(nst[s], gk[...], preferred_element_type=F32).reshape(4, 4, CHUNK, HALF)
-
-        def read(i):
-            return gt[i // 4, i % 4]
-
-        def write(i, v):
-            q[ph, s, i // 4, i % 4] = v
-
-        sc[ph, s] = quantize(read, write, 16)
+
+        def rows320(i, carry):
+            rows = pl.ds(pl.multiple_of(i * 320, 320), 320)
+            v = jnp.dot(nst[s, rows, :], gk[...], preferred_element_type=F32)
+            top = jnp.maximum(top_of(v), 1e-30)
+            q[ph, s, i] = to_i16(v * (TOP / top)).reshape(4, CHUNK, HALF)
+            sc[ph, s, i] = top / TOP
+            return carry
+
+        lax.fori_loop(0, 4, rows320, 0)
         if d < 4:
-            one = copy(q.at[ph, s, :, :, ROWS[0]], r1x.at[ph, d - 1], at_x(d), base1[ph] + d - 1, base1[ph] + d - 1)
-            one.start()
-            pending.append(one)
+            send(q.at[ph, s, :, :, ROWS[0]], r1x.at[ph, d - 1], at_x(d), base1[ph])
+        for e in (1, 2, 3):
+            send(q.at[ph, s, (y + e) % 4, :, ROWS[1]], r1y.at[ph, e - 1, s], at_y(e), base1[ph] + 1)
+            send(q.at[ph, s, :, (zl + e) % 4, ROWS[2]], r1z.at[ph, e - 1, s], at_line(e), base1[ph] + 2)
 
     def grads_send(ph):
-        for d in (1, 2, 3):
-            k = base1[ph] + 2 + d
-            one = copy(q.at[ph, :, (y + d) % 4, :, ROWS[1]], r1y.at[ph, d - 1], at_y(d), k, k)
-            one.start()
-            pending.append(one)
-            k = base1[ph] + 5 + d
-            one = copy(q.at[ph, :, :, (zl + d) % 4, ROWS[2]], r1z.at[ph, d - 1], at_line(d), k, k)
-            one.start()
-            pending.append(one)
         for a, hop in enumerate((at_x, at_y, at_line)):
-            for d in (1, 2, 3):
-                k = base1s[ph] + 3 * a + d - 1
-                one = copy(sc.at[ph], s1.at[ph, a, d - 1], hop(d), k, k)
-                one.start()
-                pending.append(one)
+            for e in (1, 2, 3):
+                send(sc.at[ph], s1.at[ph, a, e - 1], hop(e), base1[ph] + 3 + a)
 
     def wait1(ph, a, ref):
-        for d in range(3):
-            arrived(ref.at[ph, d], base1[ph] + 3 * a + d)
-            arrived(s1.at[ph, a, d], base1s[ph] + 3 * a + d)
+        arrived(ref.at[ph], base1[ph] + a)
+        arrived(s1.at[ph, a], base1[ph] + 3 + a)
 
     def i2f(v):
         return v.astype(jnp.int32).astype(F32)
 
     def stage2(ph):
         ids = {}
-        wait1(ph, 0, r1x)
-
-        def add0(i, carry):
-            a, b = i // 4, i % 4
-            v = i2f(q[ph, x, a, b, ROWS[0]]) * sc[ph, x]
-            for d in range(3):
-                v = v + i2f(r1x[ph, d, a, b]) * s1[ph, 0, d, x]
-            acc[a, b] = v
-            return carry
-
-        lax.fori_loop(0, 16, add0, 0)
-
-        def write0(i, v):
-            q2x[ph, i // 4, i % 4] = v
-
-        s2o[ph, 0] = quantize(lambda i: acc[i // 4, i % 4], write0, 16)
-        for d in (1, 2, 3):
-            ids[0, d] = (
-                send(q2x.at[ph, (y + d) % 4], r2x.at[ph, d - 1], at_y(d)),
-                send(s2o.at[ph, 0], s2.at[ph, 0, d - 1], at_y(d)),
-            )
-        wait1(ph, 1, r1y)
-
-        def add1(i, carry):
-            a, b = i // 4, i % 4
-            v = i2f(q[ph, a, y, b, ROWS[1]]) * sc[ph, a]
-            for d in range(3):
-                v = v + i2f(r1y[ph, d, a, b]) * s1[ph, 1, d, a]
-            acc[a, b] = v
-            return carry
-
-        lax.fori_loop(0, 16, add1, 0)
-
-        def write1(i, v):
-            q2y[ph, i // 4, i % 4] = v
-
-        s2o[ph, 1] = quantize(lambda i: acc[i // 4, i % 4], write1, 16)
-        for d in (1, 2, 3):
-            ids[1, d] = (
-                send(q2y.at[ph, (x + d) % 4], r2y.at[ph, d - 1], at_x(d)),
-                send(s2o.at[ph, 1], s2.at[ph, 1, d - 1], at_x(d)),
-            )
-        wait1(ph, 2, r1z)
-
-        def add2(i, carry):
-            a, b = i // 4, i % 4
-            v = i2f(q[ph, a, b, zl, ROWS[2]]) * sc[ph, a]
-            for d in range(3):
-                v = v + i2f(r1z[ph, d, a, b]) * s1[ph, 2, d, a]
-            acc[a, b, 0:16] = v
-            return carry
-
-        lax.fori_loop(0, 16, add2, 0)
-
-        def write2(i, v):
-            q2z[ph, i // 4, i % 4] = v
-
-        s2o[ph, 2] = quantize(lambda i: acc[i // 4, i % 4, 0:16], write2, 16)
-        for d in (1, 2, 3):
-            ids[2, d] = (
-                send(q2z.at[ph, (x + d) % 4], r2z.at[ph, d - 1], at_x(d)),
-                send(s2o.at[ph, 2], s2.at[ph, 2, d - 1], at_x(d)),
-            )
+        for a, (own, own_scale, got, got_scale, mid, into, pos, hop, n) in enumerate((
+            (lambda i: q[ph, x, i, :, ROWS[0]], lambda i: sc[ph, x, i],
+             r1x, lambda d, i: s1[ph, 0, d, x, i], q2x, r2x, y, at_y, 32),
+            (lambda i: q[ph, i, y, :, ROWS[1]], lambda i: sc[ph, i, y],
+             r1y, lambda d, i: s1[ph, 1, d, i, y], q2y, r2y, x, at_x, 32),
+            (lambda i: q[ph, i, :, zl, ROWS[2]], lambda i: sc[ph, i],
+             r1z, lambda d, i: s1[ph, 2, d, i], q2z, r2z, x, at_x, 16),
+        )):
+            wait1(ph, a, got)
+
+            def add(i, top):
+                v = i2f(own(i)) * own_scale(i)
+                for d in range(3):
+                    v = v + i2f(got[ph, d, i]) * got_scale(d, i)
+                acc[i, :, 0:n] = v
+                return jnp.maximum(top, top_of(v))
+
+            top = lax.fori_loop(0, 4, add, jnp.full((1, HALF), 1e-30, F32))
+            factor = TOP / top
+
+            def store(i, carry):
+                mid[ph, i] = to_i16(acc[i, :, 0:n] * factor)
+                return carry
+
+            lax.fori_loop(0, 4, store, 0)
+            s2o[ph, a] = top / TOP
+            ids[a] = (take(), take())
+            for d in (1, 2, 3):
+                send(mid.at[ph, (pos + d) % 4], into.at[ph, d - 1], hop(d), ids[a][0])
+                send(s2o.at[ph, a], s2.at[ph, a, d - 1], hop(d), ids[a][1])
         return ids
 
     def stage3(ph, ids):
         out = {}
-        for a, (own, got, mid, pos, hop, n) in enumerate((
-            (q2x.at[ph, y], r2x, q3x, zl, at_line, 32),
-            (q2y.at[ph, x], r2y, q3y, zl, at_line, 32),
-            (q2z.at[ph, x], r2z, q3z, y, at_y, 16),
+        for a, (own, got, mid, into, pos, hop) in enumerate((
+            (q2x.at[ph, y], r2x, q3x, r3x, zl, at_line),
+            (q2y.at[ph, x], r2y, q3y, r3y, zl, at_line),
+            (q2z.at[ph, x], r2z, q3z, r3z, y, at_y),
         )):
+            arrived(got.at[ph], ids[a][0])
+            arrived(s2.at[ph, a], ids[a][1])
+            v = i2f(own[...]) * s2o[ph, a]
+            for d in range(3):
+                v = v + i2f(got[ph, d]) * s2[ph, a, d]
+            top = jnp.maximum(top_of(v), 1e-30)
+            mid[ph] = to_i16(v * (TOP / top))
+            s3o[ph, a] = top / TOP
+            out[a] = (take(), take())
             for d in (1, 2, 3):
-                arrived(got.at[ph, d - 1], ids[a, d][0])
-                arrived(s2.at[ph, a, d - 1], ids[a, d][1])
-            for b in range(4):
-                v = i2f(own[b]) * s2o[ph, a]
-                for d in range(3):
-                    v = v + i2f(got[ph, d, b]) * s2[ph, a, d]
-                acc[0, b, 0:n] = v
-
-            def write(i, v, mid=mid):
-                mid[ph, i] = v
-
-            s3o[ph, a] = quantize(lambda i, n=n: acc[0, i, 0:n], write, 4)
-            into = (r3x, r3y, r3z)[a]
-            for d in (1, 2, 3):
-                out[a, d] = (
-                    send(mid.at[ph, (pos + d) % 4], into.at[ph, d - 1], hop(d)),
-                    send(s3o.at[ph, a], s3.at[ph, a, d - 1], hop(d)),
-                )
+                send(mid.at[ph, (pos + d) % 4], into.at[ph, d - 1], hop(d), out[a][0])
+                send(s3o.at[ph, a], s3.at[ph, a, d - 1], hop(d), out[a][1])
         return out
 
     def finish(ph, ids):
@@ -460,39 +408,37 @@
             (q3x.at[ph, zl], r3x, 32, 0), (q3y.at[ph, zl], r3y, 32, 32), (q3z.at[ph, y], r3z, 16, 64),
         )):
             v = i2f(own[...]) * s3o[ph, a]
-            for d in (1, 2, 3):
-                arrived(got.at[ph, d - 1], ids[a, d][0])
-                arrived(s3.at[ph, a, d - 1], ids[a, d][1])
-                v = v + i2f(got[ph, d - 1]) * s3[ph, a, d - 1]
+            arrived(got.at[ph], ids[a][0])
+            arrived(s3.at[ph, a], ids[a][1])
+            for d in range(3):
+                v = v + i2f(got[ph, d]) * s3[ph, a, d]
             grad[row : row + n, HALF * ph : HALF * ph + HALF] = v
 
     def stat_send(a, hop):
-        return [send(stat4.at[4 * a], stat4.at[4 * a + d], hop(d)) for d in (1, 2, 3)]
-
-    def stat_add(a, ids):
-        v = stat4[4 * a]
+        ri = take()
         for d in (1, 2, 3):
-            arrived(stat4.at[4 * a + d], ids[d - 1])
-            v = v + stat4[4 * a + d]
-        return v
-
-    def together(events, pieces):
-        pieces = list(pieces)
-        for _ in events:
-            if pieces:
-                pieces.pop(0)()
-        for one in pieces:
-            one()
+            send(stat4.at[4 * a], stat4.at[4 * a + d], hop(d), ri)
+        return ri
+
+    def stat_add(a, ri):
+        arrived(stat4.at[pl.ds(4 * a + 1, 3)], ri)
+        return stat4[4 * a] + stat4[4 * a + 1] + stat4[4 * a + 2] + stat4[4 * a + 3]
 
     for one in loads:
         one.wait()
-    one_a, one_b = gather(0), gather(1)
-    next(one_a)
+    first, second = gather(0), gather(1)
+    next(first)
     share_gains()
-    next(one_a)
-    next(one_b)
+    next(first)
     stat4[0] = jnp.zeros((8, HD), F32)
-    together(one_a, [wait_inputs] + [lambda t=t: prep(t) for t in range(6)] + [lambda: next(one_b)])
+    pieces = [wait_inputs] + [lambda t=t: prep(t) for t in range(6)]
+    step = 0
+    for _ in first:
+        if pieces:
+            pieces.pop(0)()
+        step += 1
+        if step >= LEAD:
+            next(second)
 
     def work(ph):
         for which in (0, 1):
@@ -503,37 +449,47 @@
             yield lambda d=d: grads(ph, d)
         yield lambda: grads_send(ph)
 
-    together(one_b, work(0))
-    for one in work(1):
+    pieces = list(work(0))
+    for _ in second:
+        if pieces:
+            pieces.pop(0)()
+    for one in pieces:
+        one()
+    pieces = list(work(1))
+    for one in pieces[:9]:
         one()
     sid = stat_send(0, at_x)
     ids_a = stage2(0)
+    for one in pieces[9:11]:
+        one()
     stat4[4] = stat_add(0, sid)
     sid = stat_send(1, at_y)
+    for one in pieces[11:12]:
+        one()
     ids_a = stage3(0, ids_a)
-    ids_b = stage2(1)
+    for one in pieces[12:]:
+        one()
     stat4[8] = stat_add(1, sid)
     sid = stat_send(2, at_line)
     finish(0, ids_a)
-    ids_b = stage3(1, ids_b)
+    ids_b = stage2(1)
     total = stat_add(2, sid)
     loss = jnp.sum(total[0:1], axis=-1, keepdims=True) / float(TOK * 64 * KW)
+    ids_b = stage3(1, ids_b)
     stats[...] = jnp.concatenate([jnp.broadcast_to(loss, (1, HD)), total[1:8]], axis=0)
     finish(1, ids_b)
-    for one in pending:
+    for one in pending.values():
         one.wait_send()
 
 
 def local(hidden_in, gain_in, w_key, key_gain, partner):
-    gains = jnp.concatenate(
-        [gain_in.astype(F32).reshape(4, 1, SLAB), jnp.pad(key_gain.astype(F32), ((0, 0), (0, SLAB - HD))).reshape(1, 1, SLAB)]
-    )
     vmem, dma = pltpu.VMEM, pltpu.SemaphoreType.DMA
     grad, stats = pl.pallas_call(
         kernel,
         out_shape=(jax.ShapeDtypeStruct((CHUNK, KW), F32), jax.ShapeDtypeStruct((8, HD), F32)),
         in_specs=[
             pl.BlockSpec(memory_space=pl.ANY),
+            pl.BlockSpec(memory_space=pltpu.VMEM),
             pl.BlockSpec(memory_space=pltpu.VMEM),
             pl.BlockSpec(memory_space=pl.ANY),
             pl.BlockSpec(memory_space=pltpu.SMEM),
@@ -548,15 +504,14 @@
             vmem((TOK, HALF), F32),
             vmem((TOK, HALF), F32),
             vmem((TOK, HALF), BF16),
-            vmem((4, 4, CHUNK, HALF), F32),
             vmem((2, 4, 4, 4, CHUNK, HALF), I16),
-            vmem((2, 4, 1, HALF), F32),
+            vmem((2, 4, 4, 1, HALF), F32),
             vmem((4, 5, 1, SLAB), F32),
             vmem((12, 8, HD), F32),
             vmem((2, 3, 4, 4, 32, HALF), I16),
             vmem((2, 3, 4, 4, 32, HALF), I16),
             vmem((2, 3, 4, 4, 16, HALF), I16),
-            vmem((2, 3, 3, 4, 1, HALF), F32),
+            vmem((2, 3, 3, 4, 4, 1, HALF), F32),
             vmem((4, 4, 32, HALF), F32),
             vmem((2, 4, 4, 32, HALF), I16),
             vmem((2, 4, 4, 32, HALF), I16),
@@ -574,7 +529,7 @@
             vmem((2, 3, 16, HALF), I16),
             vmem((2, 3, 1, HALF), F32),
             vmem((2, 3, 3, 1, HALF), F32),
-            dma((NSEM,)),
+            dma((NSEND,)),
             dma((NSEM,)),
             dma((8,)),
         ],
@@ -582,7 +537,7 @@
             collective_id=0, has_side_effects=True, vmem_limit_bytes=63 * 2**20
         ),
         cost_estimate=pl.CostEstimate(flops=12 * 10**9, bytes_accessed=10**7, transcendentals=0),
-    )(hidden_in, gains, w_key, partner)
+    )(hidden_in, gain_in, key_gain, w_key, partner)
     return (grad[None], stats[1:2], stats[0, 0:1])
 
 

time: 150 us -> 129 us (0.86)
  Pallas kernels: 142 us -> 123 us
    pallas_call x1, Pallas kernels: 142 us -> 123 us  [local(): pl.pallas_call(kernel, out_shape=(jax.ShapeDtypeStruct((CHUNK, KW), F32),...]
where the time goes in v2:
time: 129 us; the launch traced here: 128 us
  Pallas kernels  123 us (95%)
  local copies, waits for them, and re-layouts  3.98 us (3%)
    pallas_call x1, Pallas kernels, local(): pl.pallas_call(kernel, out_shape=(jax.ShapeDtypeStruct((CHUNK, KW), F32),...  123 us

profile of v2, /device:TPU:8, one launch (start us, length us, event | category | flops | bytes accessed | tf_op | source)
XLA Modules:
  0.0 127.8 jit_solution(9527402844074792890)
XLA Ops:
  0.6 123.2 %shard_map.76 = (f32[80,512]{1,0:T(8,128)}, f32[8,128]{1,0:T(8,128)}) custom-call(bf16[1,768,5120]{2,1,0:T(8,128)(2,1)} %hid.1, bf16[1,5120]{1,0:T(2,128)(2,1)} %gain.1, bf16[1,128]{1,0:T(2,128)(2,1)} %key_gain.1, bf16[1,80,512]{2,1,0:T(8,128)(2,1)} %w.1, s32[4]{0:T(128)} %partner.1), custom_call_target="tpu_custom_call" | custom-call | flops 12000000000 | bytes 10000000 | tf_op jit(solution)/shard_map/pallas_call | solution.py:487
  123.8 1.2 slice.7
  125.0 1.2 slice.6
  126.2 1.6 %copy.9 = f32[1,80,512]{2,1,0:T(8,128)} copy(f32[1,80,512]{2,1,0:T(8,128)} %bitcast.2) | data formatting | bytes 327680

commit v3 on v2

--- a/solution.py
+++ b/solution.py
@@ -123,11 +123,13 @@
         at = (at_x, at_y)
         pos = (x, y)
 
-        first = []
-        for part, hop in ((0, at_y), (1, at_x), (2, at_x)):
-            mine = chunk(x, y, part)
-            first.append([send(mine, mine, hop(d)) for d in (1, 2, 3)])
-        yield
+        first = {}
+
+        def start(*parts):
+            for part in parts:
+                mine = chunk(x, y, part)
+                hop = at_y if part == 0 else at_x
+                first[part] = [send(mine, mine, hop(d)) for d in (1, 2, 3)]
 
         ring = {}
         last = {}
@@ -182,54 +184,66 @@
             arrived(block(part, zz, pos[part] + 2, 1), down)
             hand_over(part, j)
 
-        for d in (1, 2, 3):
-            arrived(chunk(x, (y - d + 4) % 4, 0), first[0][d - 1])
-        z_own(0, x)
-        l_own(0, 0)
-        for d in (1, 2, 3):
-            arrived(chunk((x - d + 4) % 4, y, 1), first[1][d - 1])
-        z_own(1, y)
-        l_own(1, 0)
-        for d in (1, 2, 3):
-            arrived(chunk((x - d + 4) % 4, y, 2), first[2][d - 1])
-        mine = walls[ph].at[m, :, y, zl, ROWS[2]]
-        second = [send(mine, mine, at_y(d)) for d in (1, 2, 3)]
-        yield
-        for j in range(1, 5):
-            for part in (0, 1):
-                z_step(part, pos[part], j)
-                for sign in (-1, 1) if j < 4 else (1,):
-                    l_own(part, sign * j)
-                yield
-            if j == 1:
-                for d in (1, 2, 3):
-                    arrived(walls[ph].at[m, :, (y - d + 4) % 4, zl, ROWS[2]], second[d - 1])
-                z_own(2, None)
-                hand_over(2, 0)
-            else:
-                z_step(2, None, j - 1)
-                hand_over(2, j - 1)
-                hand_over(2, 1 - j)
-            yield
-            for part in (0, 1):
-                for sign in (-1, 1) if j > 1 else (1,):
-                    l_pass(part, sign * (j - 1))
-                if j > 1:
-                    for sign in (-1, 1) if j > 2 else (1,):
-                        l_end(part, sign * (j - 2))
-                yield
-        for part in (0, 1):
+        second = []
+
+        def z_second():
+            for d in (1, 2, 3):
+                arrived(chunk((x - d + 4) % 4, y, 2), first[2][d - 1])
+            mine = walls[ph].at[m, :, y, zl, ROWS[2]]
+            second.extend(send(mine, mine, at_y(d)) for d in (1, 2, 3))
+
+        def z_third():
+            for d in (1, 2, 3):
+                arrived(walls[ph].at[m, :, (y - d + 4) % 4, zl, ROWS[2]], second[d - 1])
+            z_own(2, None)
+            hand_over(2, 0)
+
+        def z_ring(j):
+            z_step(2, None, j)
+            hand_over(2, j)
+            if j < 4:
+                hand_over(2, -j)
+
+        def own(part):
+            for d in (1, 2, 3):
+                arrived((chunk(x, (y - d + 4) % 4, 0), chunk((x - d + 4) % 4, y, 1))[part], first[part][d - 1])
+            z_own(part, pos[part])
+            l_own(part, 0)
+
+        def ring_step(part, j):
+            z_step(part, pos[part], j)
+            for sign in (-1, 1) if j < 4 else (1,):
+                l_own(part, sign * j)
+
+        def line_step(part, j):
+            for sign in (-1, 1) if j > 1 else (1,):
+                l_pass(part, sign * (j - 1))
+            if j > 1:
+                for sign in (-1, 1) if j > 2 else (1,):
+                    l_end(part, sign * (j - 2))
+
+        def near(part):
             l_pass(part, 4)
             for sign in (-1, 1):
                 l_end(part, sign * 3)
-            yield
-        z_step(2, None, 4)
-        hand_over(2, 4)
-        for part in (0, 1):
+
+        def far(part):
             l_end(part, 4)
-        yield
-        for h in range(2):
-            arrived(walls[ph].at[h * 2 + 1 - c], back + h)
+
+        def whole():
+            for h in range(2):
+                arrived(walls[ph].at[h * 2 + 1 - c], back + h)
+
+        zs = [z_second, z_third] + [lambda j=j: z_ring(j) for j in (1, 2, 3, 4)]
+        js = [
+            [lambda j=j, part=part: ring_step(part, j) for part in (0, 1)]
+            + [lambda j=j, part=part: line_step(part, j) for part in (0, 1)]
+            for j in (1, 2, 3, 4)
+        ]
+        return (
+            start, [lambda part=part: own(part) for part in (0, 1)], zs, js,
+            [lambda part=part: near(part) for part in (0, 1)], [lambda part=part: far(part) for part in (0, 1)], whole,
+        )
 
     def teacher():
         return partner[m]
@@ -248,7 +262,7 @@
 
     def prep(t):
         def rows16(i, carry):
-            rows = pl.ds(pl.multiple_of(t * 128 + i * 16, 16), 16)
+            rows = pl.ds(pl.multiple_of(t * 64 + i * 16, 16), 16)
             total = jnp.zeros((16, 1), F32)
             for s in range(4):
                 v = nt[s, rows, :].astype(F32)
@@ -261,8 +275,9 @@
                 nt[s, rows, :] = (v * g4[p, s]).astype(BF16)
             return carry
 
-        lax.fori_loop(0, 8, rows16, 0)
-
+        lax.fori_loop(0, 4, rows16, 0)
+
+    def transpose(t):
         def turn(s, carry):
             nst[s, :, pl.ds(t * 128, 128)] = ns[s, pl.ds(t * 128, 128), :].T
             return carry
@@ -330,11 +345,20 @@
             return carry
 
         lax.fori_loop(0, 4, rows320, 0)
+        if ph == 0:
+            return
         if d < 4:
             send(q.at[ph, s, :, :, ROWS[0]], r1x.at[ph, d - 1], at_x(d), base1[ph])
         for e in (1, 2, 3):
             send(q.at[ph, s, (y + e) % 4, :, ROWS[1]], r1y.at[ph, e - 1, s], at_y(e), base1[ph] + 1)
             send(q.at[ph, s, :, (zl + e) % 4, ROWS[2]], r1z.at[ph, e - 1, s], at_line(e), base1[ph] + 2)
+
+    def send_all(ph):
+        for e in (1, 2, 3):
+            send(q.at[ph, (x + e) % 4, :, :, ROWS[0]], r1x.at[ph, e - 1], at_x(e), base1[ph])
+            send(q.at[ph, :, (y + e) % 4, :, ROWS[1]], r1y.at[ph, e - 1], at_y(e), base1[ph] + 1)
+            send(q.at[ph, :, :, (zl + e) % 4, ROWS[2]], r1z.at[ph, e - 1], at_line(e), base1[ph] + 2)
+        grads_send(ph)
 
     def grads_send(ph):
         for a, hop in enumerate((at_x, at_y, at_line)):
@@ -426,49 +450,74 @@
 
     for one in loads:
         one.wait()
-    first, second = gather(0), gather(1)
-    next(first)
+    start_a, own_a, z_a, j_a, near_a, far_a, whole_a = gather(0)
+    start_b, own_b, z_b, j_b, near_b, far_b, whole_b = gather(1)
+    stat4[0] = jnp.zeros((8, HD), F32)
+    start_a(2, 0, 1)
+    start_b(2)
     share_gains()
-    next(first)
-    stat4[0] = jnp.zeros((8, HD), F32)
-    pieces = [wait_inputs] + [lambda t=t: prep(t) for t in range(6)]
-    step = 0
-    for _ in first:
-        if pieces:
-            pieces.pop(0)()
-        step += 1
-        if step >= LEAD:
-            next(second)
 
     def work(ph):
-        for which in (0, 1):
-            for s in range(4):
-                yield lambda which=which, s=s: keys(ph, which, s)
-        yield lambda: distill(ph)
-        for d in (1, 2, 3, 4):
-            yield lambda d=d: grads(ph, d)
-        yield lambda: grads_send(ph)
-
-    pieces = list(work(0))
-    for _ in second:
-        if pieces:
-            pieces.pop(0)()
-    for one in pieces:
+        return (
+            [lambda s=s: keys(ph, 0, s) for s in range(4)],
+            [lambda s=s: keys(ph, 1, s) for s in range(4)] + [lambda: distill(ph)],
+            [lambda d=d: grads(ph, d) for d in (1, 2, 3, 4)],
+        )
+
+    def woven(events, pieces):
+        done = 0
+        for k, event in enumerate(events):
+            event()
+            upto = (k + 1) * len(pieces) // len(events)
+            for one in pieces[done:upto]:
+                one()
+            done = upto
+
+    student_a, teacher_a, grads_a = work(0)
+    student_b, teacher_b, grads_b = work(1)
+    a = [z_a[0]] + own_a + [z_a[1], z_b[0]] + j_a[0] + [z_a[2], z_b[1]] + j_a[1] + [z_a[3], lambda: start_b(0, 1)]
+    woven(a, [wait_inputs] + [
+        lambda do=do, t=t: do(t) for k in range(6) for do, t in ((prep, 2 * k), (prep, 2 * k + 1), (transpose, k))
+    ])
+    a = j_a[2] + [z_a[4]] + j_a[3] + near_a + [z_a[5]] + far_a
+    b = own_b + [z_b[2]] + j_b[0] + [z_b[3]] + j_b[1]
+    early = LEAD
+    for one in a[: len(a) - early]:
         one()
-    pieces = list(work(1))
-    for one in pieces[:9]:
+    mixed = []
+    rest = a[len(a) - early :]
+    while rest:
+        mixed.append(rest.pop(0))
+        if b:
+            mixed.append(b.pop(0))
+    b = b + [z_b[4]] + j_b[2] + j_b[3] + near_b
+    cut = mixed.index(near_a[1]) + 1
+    woven(mixed[:cut], [])
+    woven(mixed[cut:], student_a)
+    b[0]()
+    whole_a()
+    woven(b[1:], teacher_a + grads_a)
+    send_all(0)
+    student_b[0]()
+    student_b[1]()
+    z_b[5]()
+    for one in far_b:
+        one()
+    student_b[2]()
+    student_b[3]()
+    whole_b()
+    for one in teacher_b:
         one()
     sid = stat_send(0, at_x)
+    grads_b[0]()
+    grads_b[1]()
     ids_a = stage2(0)
-    for one in pieces[9:11]:
-        one()
+    grads_b[2]()
     stat4[4] = stat_add(0, sid)
     sid = stat_send(1, at_y)
-    for one in pieces[11:12]:
-        one()
+    grads_b[3]()
+    grads_send(1)
     ids_a = stage3(0, ids_a)
-    for one in pieces[12:]:
-        one()
     stat4[8] = stat_add(1, sid)
     sid = stat_send(2, at_line)
     finish(0, ids_a)

time: 129 us -> 124 us (0.961)
  Pallas kernels: 123 us -> 119 us
    pallas_call x1, Pallas kernels: 123 us -> 119 us  [local(): pl.pallas_call(kernel, out_shape=(jax.ShapeDtypeStruct((CHUNK, KW), F32),...]
where the time goes in v3:
time: 124 us
  Pallas kernels  119 us (96%)
  local copies, waits for them, and re-layouts  3.98 us (3%)
    pallas_call x1, Pallas kernels, local(): pl.pallas_call(kernel, out_shape=(jax.ShapeDtypeStruct((CHUNK, KW), F32),...  119 us

profile of v3, /device:TPU:8, one launch (start us, length us, event | category | flops | bytes accessed | tf_op | source)
XLA Modules:
  0.0 123.9 jit_solution(11008939762661049321)
XLA Ops:
  0.6 119.3 %shard_map.76 = (f32[80,512]{1,0:T(8,128)}, f32[8,128]{1,0:T(8,128)}) custom-call(bf16[1,768,5120]{2,1,0:T(8,128)(2,1)} %hid.1, bf16[1,5120]{1,0:T(2,128)(2,1)} %gain.1, bf16[1,128]{1,0:T(2,128)(2,1)} %key_gain.1, bf16[1,80,512]{2,1,0:T(8,128)(2,1)} %w.1, s32[4]{0:T(128)} %partner.1), custom_call_target="tpu_custom_call" | custom-call | flops 12000000000 | bytes 10000000 | tf_op jit(solution)/shard_map/pallas_call | solution.py:536
  119.9 1.2 slice.7
  121.1 1.2 slice.6
  122.3 1.6 %copy.9 = f32[1,80,512]{2,1,0:T(8,128)} copy(f32[1,80,512]{2,1,0:T(8,128)} %bitcast.2) | data formatting | bytes 327680

commit v4 on v3

--- a/solution.py
+++ b/solution.py
@@ -13,7 +13,7 @@
 EPS = 1e-6
 TOP = 32767.0
 ROWS = (pl.ds(0, 32), pl.ds(32, 32), pl.ds(64, 16))
-NSEM = 250
+NSEM = 254
 NSEND = 96
 LEAD = 10
 MAGIC = 12582912.0
@@ -21,7 +21,7 @@
 
 def kernel(
     hid, gain, key_gain, w, partner, grad, stats,
-    wall0, wall1, ns, nt, nst, ks, kt, gk, q, sc, g4, stat4,
+    wall0, wall1, ns, nt, nst, ks, kt, gk, q, sc, g4, gz, stat4,
     r1x, r1y, r1z, s1, acc, q2x, q2y, q2z, r2x, r2y, r2z, s2o, s2,
     q3x, q3y, q3z, r3x, r3y, r3z, s3o, s3, ssem, rsem, lsem,
 ):
@@ -48,8 +48,7 @@
 
     walls = (wall0, wall1)
     sibling = dev(x, y, z, 1 - c)
-    others = (sibling, dev(x, y, z + 4, c), dev(x, y, z + 4, 1 - c))
-    slot_of = (zh * 2 + 1 - c, (1 - zh) * 2 + c, (1 - zh) * 2 + 1 - c)
+    far_half = (1 - zh) * 2 + c
 
     used, sent = [0], [0]
     pending = {}
@@ -92,7 +91,7 @@
         one.start()
     barrier = pltpu.get_barrier_semaphore()
     peers = [at_x(d) for d in (1, 2, 3)] + [at_y(d) for d in (1, 2, 3)] + [at_z(1), at_z(-1)]
-    peers += [at_line(d) for d in (1, 2, 3)] + list(others)
+    peers += [at_line(d) for d in (1, 2, 3)] + [sibling]
     for one in peers:
         pl.semaphore_signal(barrier, inc=1, device_id=one, device_id_type=MESH)
     for s in range(4):
@@ -251,12 +250,25 @@
     got_gain = []
 
     def share_gains():
-        for to in others:
-            got_gain.append(send(g4.at[m], g4.at[m], to))
+        got_gain.append(send(g4.at[m], gz.at[0], at_z(1)))
+        got_gain.append(send(g4.at[m], gz.at[1], at_z(-1)))
+
+    def pass_gains():
+        arrived(gz.at[0], got_gain[0])
+        got_gain.append(send(gz.at[0], gz.at[2], at_z(1)))
+        arrived(gz.at[1], got_gain[1])
+        got_gain.append(send(gz.at[1], gz.at[4], at_z(-1)))
+
+    def hand_gains():
+        arrived(gz.at[2], got_gain[2])
+        arrived(gz.at[4], got_gain[3])
+        g4[far_half] = gz[(zl * 2) % 5]
+        got_gain.append(send(g4.at[m], g4.at[m], sibling))
+        got_gain.append(send(g4.at[far_half], g4.at[far_half], sibling))
 
     def wait_inputs():
-        for slot, ri in zip(slot_of, got_gain):
-            arrived(g4.at[slot], ri)
+        arrived(g4.at[zh * 2 + 1 - c], got_gain[4])
+        arrived(g4.at[(1 - zh) * 2 + 1 - c], got_gain[5])
         for one in hidden_loads:
             one.wait()
 
@@ -476,14 +488,11 @@
     student_a, teacher_a, grads_a = work(0)
     student_b, teacher_b, grads_b = work(1)
     a = [z_a[0]] + own_a + [z_a[1], z_b[0]] + j_a[0] + [z_a[2], z_b[1]] + j_a[1] + [z_a[3], lambda: start_b(0, 1)]
-    woven(a, [wait_inputs] + [
-        lambda do=do, t=t: do(t) for k in range(6) for do, t in ((prep, 2 * k), (prep, 2 * k + 1), (transpose, k))
-    ])
+    opening = a
     a = j_a[2] + [z_a[4]] + j_a[3] + near_a + [z_a[5]] + far_a
     b = own_b + [z_b[2]] + j_b[0] + [z_b[3]] + j_b[1]
     early = LEAD
-    for one in a[: len(a) - early]:
-        one()
+    opening = opening + a[: len(a) - early]
     mixed = []
     rest = a[len(a) - early :]
     while rest:
@@ -492,7 +501,9 @@
             mixed.append(b.pop(0))
     b = b + [z_b[4]] + j_b[2] + j_b[3] + near_b
     cut = mixed.index(near_a[1]) + 1
-    woven(mixed[:cut], [])
+    woven(opening + mixed[:cut], [pass_gains, hand_gains, wait_inputs] + [
+        lambda do=do, t=t: do(t) for k in range(6) for do, t in ((prep, 2 * k), (prep, 2 * k + 1), (transpose, k))
+    ])
     woven(mixed[cut:], student_a)
     b[0]()
     whole_a()
@@ -556,6 +567,7 @@
             vmem((2, 4, 4, 4, CHUNK, HALF), I16),
             vmem((2, 4, 4, 1, HALF), F32),
             vmem((4, 5, 1, SLAB), F32),
+            vmem((5, 5, 1, SLAB), F32),
             vmem((12, 8, HD), F32),
             vmem((2, 3, 4, 4, 32, HALF), I16),
             vmem((2, 3, 4, 4, 32, HALF), I16),

time: 124 us -> 122 us (0.984)
  Pallas kernels: 119 us -> 117 us
    pallas_call x1, Pallas kernels: 119 us -> 117 us  [local(): pl.pallas_call(kernel, out_shape=(jax.ShapeDtypeStruct((CHUNK, KW), F32),...]
where the time goes in v4:
time: 122 us
  Pallas kernels  117 us (96%)
  local copies, waits for them, and re-layouts  3.98 us (3%)
    pallas_call x1, Pallas kernels, local(): pl.pallas_call(kernel, out_shape=(jax.ShapeDtypeStruct((CHUNK, KW), F32),...  117 us

profile of v4, /device:TPU:8, one launch (start us, length us, event | category | flops | bytes accessed | tf_op | source)
XLA Modules:
  0.0 121.8 jit_solution(3106857749478887863)
XLA Ops:
  0.6 117.2 %shard_map.76 = (f32[80,512]{1,0:T(8,128)}, f32[8,128]{1,0:T(8,128)}) custom-call(bf16[1,768,5120]{2,1,0:T(8,128)(2,1)} %hid.1, bf16[1,5120]{1,0:T(2,128)(2,1)} %gain.1, bf16[1,128]{1,0:T(2,128)(2,1)} %key_gain.1, bf16[1,80,512]{2,1,0:T(8,128)(2,1)} %w.1, s32[4]{0:T(128)} %partner.1), custom_call_target="tpu_custom_call" | custom-call | flops 12000000000 | bytes 10000000 | tf_op jit(solution)/shard_map/pallas_call | solution.py:547
  117.8 1.2 slice.7
  119.0 1.2 slice.6
  120.2 1.6 %copy.9 = f32[1,80,512]{2,1,0:T(8,128)} copy(f32[1,80,512]{2,1,0:T(8,128)} %bitcast.2) | data formatting | bytes 327680

commit v5 on v4

--- a/solution.py
+++ b/solution.py
@@ -521,8 +521,8 @@
         one()
     sid = stat_send(0, at_x)
     grads_b[0]()
+    ids_a = stage2(0)
     grads_b[1]()
-    ids_a = stage2(0)
     grads_b[2]()
     stat4[4] = stat_add(0, sid)
     sid = stat_send(1, at_y)

time: 122 us -> 122 us (level)
  no operation moved by 1% of the time
where the time goes in v5:
time: 122 us; the launch traced here: 121 us
  Pallas kernels  116 us (95%)
  local copies, waits for them, and re-layouts  3.98 us (3%)
    pallas_call x1, Pallas kernels, local(): pl.pallas_call(kernel, out_shape=(jax.ShapeDtypeStruct((CHUNK, KW), F32),...  116 us

profile of v5, /device:TPU:8, one launch (start us, length us, event | category | flops | bytes accessed | tf_op | source)
XLA Modules:
  0.0 120.7 jit_solution(3262727409581727138)
XLA Ops:
  0.6 116.1 %shard_map.76 = (f32[80,512]{1,0:T(8,128)}, f32[8,128]{1,0:T(8,128)}) custom-call(bf16[1,768,5120]{2,1,0:T(8,128)(2,1)} %hid.1, bf16[1,5120]{1,0:T(2,128)(2,1)} %gain.1, bf16[1,128]{1,0:T(2,128)(2,1)} %key_gain.1, bf16[1,80,512]{2,1,0:T(8,128)(2,1)} %w.1, s32[4]{0:T(128)} %partner.1), custom_call_target="tpu_custom_call" | custom-call | flops 12000000000 | bytes 10000000 | tf_op jit(solution)/shard_map/pallas_call | solution.py:547
  116.7 1.2 slice.7
  117.9 1.2 slice.6
  119.1 1.6 %copy.9 = f32[1,80,512]{2,1,0:T(8,128)} copy(f32[1,80,512]{2,1,0:T(8,128)} %bitcast.2) | data formatting | bytes 327680
